TPU v7x, 128 devices: a whole 4x4x4 slice. The times are simulated.
128 devices in a mesh: row: 8 (over x, y_lo), col: 16 (over y_hi, z, core).
Axes of the slice: x: 4, y: 4 (y_hi: 2, y_lo: 2; y = y_hi * 2 + y_lo), z: 4, core: 2. Of those that a mesh axis runs over, the one named last changes fastest.
Arguments:
- momentum: float32 [29568, 8192], P(('row', 'col')), may hold values from -100 to 100
- gradient: bfloat16 [29568, 8192], P(('row', 'col')), may hold values from -24 to 24
- right_basis: bfloat16 [8192, 512], P(('row', 'col')), may hold values from -0.0625 to 0.0625
- weight: bfloat16 [29568, 8192], P('row', 'col'), may hold values from -6 to 6
- tokens: bfloat16 [512, 29568], P('col', 'row'), may hold values from -6 to 6
Outputs:
- new_momentum: float32 [29568, 8192], P(('row', 'col'))
- new_basis: bfloat16 [8192, 512], P(('row', 'col'))
- new_weight: bfloat16 [29568, 8192], P('row', 'col')
- logits: bfloat16 [512, 8192], P('row', 'col')
All inputs are finite; a program needn't handle non-finite values.
Results may differ from a plain program's by a relative error of at most 0.02.
Values may be sent and summed in bfloat16 or wider, within the bound.
No kernel may reach another device: no remote copies, remote signals or barrier semaphores. Data moves between devices by JAX's collectives and lax.ppermute only.
A program may use at most 128 MiB of HBM per device.

v0:
```python
import math

import jax
import jax.numpy as jnp
from jax import lax
from jax.sharding import PartitionSpec as P

EPSILON = 1e-06
MOMENTUM_DECAY = 0.95
STEP_SIZE = 0.3


def contract_rows(left, right):
    return lax.dot_general(
        left, right, (((0,), (0,)), ((), ())), preferred_element_type=jnp.float32
    )


def contract_cols(left, right):
    return lax.dot_general(
        left, right, (((1,), (1,)), ((), ())), preferred_element_type=jnp.float32
    )


def shards(momentum, gradient, right_basis, weight, tokens):
    row_count = lax.axis_size("row")
    col_count = lax.axis_size("col")
    devices_all = row_count * col_count
    own_index = lax.axis_index("row") * col_count + lax.axis_index("col")
    width_model = momentum.shape[1]
    basis_rank = right_basis.shape[1]
    total_rows = momentum.shape[0] * devices_all
    own_width = width_model // devices_all
    tile_width = width_model // col_count
    buffer = momentum + gradient.astype(jnp.float32)
    buffer_low = buffer.astype(jnp.bfloat16)
    columns = buffer_low
    projected = jnp.dot(
        columns,
        lax.all_gather(right_basis, ("row", "col"), axis=0, tiled=True),
        preferred_element_type=jnp.float32,
    )
    col_squares = lax.psum(jnp.sum(projected * projected, axis=0), ("row", "col"))
    left_factor = (projected * lax.rsqrt(col_squares + EPSILON)).astype(jnp.bfloat16)
    columns = buffer_low
    summed = lax.psum_scatter(
        contract_rows(columns, left_factor), ("row", "col"), scatter_dimension=0, tiled=True
    )
    back_low = summed.astype(jnp.bfloat16)
    back_full = lax.all_gather(back_low, ("row", "col"), axis=0, tiled=True)
    back_wide = back_full.astype(jnp.float32)
    own_wide = back_low.astype(jnp.float32)
    basis_squares = lax.psum(jnp.sum(own_wide * own_wide, axis=0), ("row", "col"))
    basis_full = (back_wide * lax.rsqrt(basis_squares + EPSILON)).astype(jnp.bfloat16)
    new_basis = lax.dynamic_slice_in_dim(basis_full, own_index * own_width, own_width, 0)
    new_momentum = buffer - (1.0 - MOMENTUM_DECAY) * contract_cols(left_factor, back_full)
    basis_tile = lax.dynamic_slice_in_dim(
        basis_full, lax.axis_index("col") * tile_width, tile_width, 0
    )
    step_scale = STEP_SIZE * math.sqrt(total_rows * width_model / basis_rank)
    change = contract_cols(lax.all_gather(left_factor, "col", axis=0, tiled=True), basis_tile)
    new_weight = (weight.astype(jnp.float32) - step_scale * change).astype(jnp.bfloat16)
    partial_logits = jnp.dot(
        lax.all_gather(tokens, "col", axis=0, tiled=True),
        new_weight,
        preferred_element_type=jnp.float32,
    )
    summed_logits = lax.psum_scatter(
        partial_logits.astype(jnp.bfloat16), "row", scatter_dimension=0, tiled=True
    ).astype(jnp.float32)
    logits = (summed_logits * total_rows ** (-0.5)).astype(jnp.bfloat16)
    return (new_momentum, new_basis, new_weight, logits)


def solution(mesh):
    in_specs = (
        P(("row", "col"), None),
        P(("row", "col"), None),
        P(("row", "col"), None),
        P("row", "col"),
        P("col", "row"),
    )
    out_specs = (P(("row", "col"), None), P(("row", "col"), None), P("row", "col"), P("row", "col"))
    return jax.shard_map(shards, mesh=mesh, in_specs=in_specs, out_specs=out_specs, check_vma=False)
```

profile of v0, /device:TPU:1, one launch (start us, length us, event | category | flops | bytes accessed | tf_op | source)
XLA Modules:
  0.0 1316.3 jit_solution(3646969252715509376)
XLA Ops:
  7.2 0.7 all-gather.6.cloned.1.call-update
  7.9 207.9 %all-gather.6.cloned.1.call-done = bf16[8192,512]{1,0:T(8,128)(2,1)} async-done(((bf16[64,512]{1,0:T(8,128)(2,1)}), bf16[8192,512]{1,0:T(8,128)(2,1)}) %all-gather.6.cloned.1.call-update) | async-done | bytes 8388624 | tf_op jit(solution)/shard_map/all_gather | solution.py:40
  215.8 8.8 multiply_reduce_fusion
  224.6 63.3 %psum.14 = f32[512]{0:T(512)S(1)} all-reduce(f32[512]{0:T(512)S(1)} %get-tuple-element.18), channel_id=1, replica_groups=mesh['row'=8,'col'=16] {'row','col'}, use_global_device_ids=true, to_apply=%region_1.0 | all-reduce | flops 512 | bytes 4096 | tf_op jit(solution)/shard_map/psum | solution.py:43
  288.0 12.5 fusion.5
  300.6 0.7 fusion.16
  301.4 0.0 all-gather.8.cloned.1.call-start
  301.4 654.0 %reduce-scatter.5.cloned.1.call-done = f32[64,512]{1,0:T(8,128)} async-done(((f32[8192,512]{1,0:T(8,128)}), f32[64,512]{1,0:T(8,128)}) %reduce-scatter.5.cloned.1.call-update) | async-done | bytes 131088 | tf_op jit(solution)/shard_map/reduce_scatter | solution.py:46
  955.4 1.5 multiply_reduce_fusion.1
  957.1 0.5 all-gather.10.cloned.1.call-update
  957.7 55.5 %all-gather.12.cloned.1.call-done = bf16[16,231,512]{2,1,0:T(8,128)(2,1)} async-done(((bf16[1,231,512]{2,1,0:T(8,128)(2,1)}), bf16[16,231,512]{2,1,0:T(8,128)(2,1)}) %all-gather.12.cloned.1.call-update) | async-done | bytes 3784720 | tf_op jit(solution)/shard_map/all_gather | solution.py:61
  1013.2 4.0 reshape.11
  1017.1 64.2 %psum.15 = f32[512]{0:T(512)S(1)} all-reduce(f32[512]{0:T(512)S(1)} %get-tuple-element.16), channel_id=1, replica_groups=mesh['row'=8,'col'=16] {'row','col'}, use_global_device_ids=true, to_apply=%region_4.0 | all-reduce | flops 512 | bytes 4096 | tf_op jit(solution)/shard_map/psum | solution.py:53
  1081.4 134.3 %all-gather.8.cloned.1.call-done = bf16[8192,512]{1,0:T(8,128)(2,1)} async-done(((bf16[64,512]{1,0:T(8,128)(2,1)}), bf16[8192,512]{1,0:T(8,128)(2,1)}) %all-gather.8.cloned.1.call-update) | async-done | bytes 8388624 | tf_op jit(solution)/shard_map/all_gather | solution.py:50
  1215.7 8.3 multiply_convert_fusion
  1223.9 1.5 constant_dynamic-slice_fusion
  1225.4 7.8 subtract_convert_fusion
  1233.2 37.7 %all-gather.10.cloned.1.call-done = bf16[512,3696]{1,0:T(8,128)(2,1)} async-done(((bf16[32,3696]{1,0:T(8,128)(2,1)}), bf16[512,3696]{1,0:T(8,128)(2,1)}) %all-gather.10.cloned.1.call-update) | async-done | bytes 3784720 | tf_op jit(solution)/shard_map/all_gather | solution.py:64
  1270.9 5.5 fusion.2
  1276.4 1.1 copy.12
  1277.5 12.3 fusion
  1289.7 18.0 %reduce-scatter.7.cloned.1.call-done = bf16[64,512]{1,0:T(8,128)(2,1)} async-done(((bf16[512,512]{1,0:T(8,128)(2,1)}), bf16[64,512]{1,0:T(8,128)(2,1)}) %reduce-scatter.7.cloned.1.call-update) | async-done | bytes 65552
  1307.7 1.0 copy.13
  1308.7 0.7 copy.11
  (12 shorter events, 0.3 us)
Async XLA Ops:
  7.2 208.6 %all-gather.6.cloned.1.call-start = ((), (), s32[]{:S(2)}) async-start(), calls=%async_computation.2 | async-start | bytes 8454144 | tf_op jit(solution)/shard_map/all_gather | solution.py:40
  7.9 947.5 %reduce-scatter.5.cloned.1.call-start = ((), (), s32[]{:S(2)}) async-start(), calls=%async_computation.3 | async-start | bytes 16908288 | tf_op jit(solution)/shard_map/reduce_scatter | solution.py:46
  300.6 712.6 %all-gather.12.cloned.1.call-start = ((), (), s32[]{:S(2)}) async-start(), calls=%async_computation.6 | async-start | bytes 4038656 | tf_op jit(solution)/shard_map/all_gather | solution.py:61
  301.4 914.3 %all-gather.8.cloned.1.call-start = ((), (), s32[]{:S(2)}) async-start(), calls=%async_computation.4 | async-start | bytes 8454144 | tf_op jit(solution)/shard_map/all_gather | solution.py:50
  957.0 313.9 %all-gather.10.cloned.1.call-start = ((), (), s32[]{:S(2)}) async-start(), calls=%async_computation.5 | async-start | bytes 4038656 | tf_op jit(solution)/shard_map/all_gather | solution.py:64
  957.6 350.1 %reduce-scatter.7.cloned.1.call-start = ((), (), s32[]{:S(2)}) async-start(), calls=%async_computation.7 | async-start | bytes 589824
Sparse Core Ops, SparseCore 0:
  9.7 206.0 all-gather.5
  300.7 654.7 reduce-scatter.4
  958.5 54.6 all-gather.11
  1015.3 200.2 all-gather.7
  1218.0 52.8 all-gather.9
  1277.6 30.0 reduce-scatter.6
where the time goes:
time: 1320 us
  waiting for transfers between devices  1110 us (84%)
  blocking collectives  128 us (10%)
  matrix products  46.9 us (4%)
  between operations  14.1 us (1%)
    reduce_scatter x1, waiting for transfers between devices, shards(): lax.psum_scatter(contract_rows(columns, left_factor), ('row', 'col'), sca...  654 us
    all_gather x1, waiting for transfers between devices, shards(): lax.all_gather(right_basis, ('row', 'col'), axis=0, tiled=True)  208 us
    all_gather x1, waiting for transfers between devices, shards(): back_full = lax.all_gather(back_low, ('row', 'col'), axis=0, tiled=True)  134 us
    psum x1, blocking collectives, shards(): lax.psum(jnp.sum(own_wide * own_wide, axis=0), ('row', 'col'))  64.2 us
    psum x1, blocking collectives, shards(): lax.psum(jnp.sum(projected * projected, axis=0), ('row', 'col'))  63.3 us
    all_gather x1, waiting for transfers between devices, shards(): lax.all_gather(left_factor, 'col', axis=0, tiled=True)  55.5 us
    all_gather x1, waiting for transfers between devices, shards(): lax.all_gather(tokens, 'col', axis=0, tiled=True)  37.7 us
  transfers between devices with their start and end apart: 6, of which 6 were waited for; matrix products, arithmetic and copies ran while one was open for 3% of the time, Pallas kernels for 0%

commit v1 on v0

v1 whole, which is shorter than its diff:
```python
import math

import jax
import jax.numpy as jnp
from jax import lax
from jax.experimental import pallas as pl
from jax.experimental.pallas import tpu as pltpu
from jax.sharding import PartitionSpec as P

EPSILON = 1e-06
MOMENTUM_DECAY = 0.95
STEP_SIZE = 0.3
BF = jnp.bfloat16
F32 = jnp.float32
ALL = ("row", "col")
VMEM_LIMIT = 48 * 1024 * 1024
HALF = 256
UNIT = 512


def device_id(x, y, z, core):
    x, y, z = x % 4, y % 4, z % 4
    return (x * 2 + y % 2) * 16 + (y // 2) * 8 + z * 2 + core


def places():
    return [(x, y, z, c) for x in range(4) for y in range(4) for z in range(4) for c in range(2)]


def moved(place, axis, shift):
    place = list(place)
    place["xyz".index(axis)] += shift
    return device_id(*place)


def shift_by(value, axes, shift):
    pairs = [(device_id(*p), moved(p, axes[p[3]], shift)) for p in places()]
    return lax.ppermute(value, ALL, pairs)


def swap_cores(value):
    return lax.ppermute(value, ALL, [(i, i ^ 1) for i in range(128)])


def gather_ring(block, axes):
    after = shift_by(block, axes, -1)
    before = shift_by(block, axes, 1)
    across = shift_by(block, axes, 2)
    return [block, after, across, before]


def scatter_ring(blocks, axes):
    from_before = shift_by(blocks[1], axes, 1)
    from_after = shift_by(blocks[3], axes, -1)
    from_across = shift_by(blocks[2], axes, 2)
    return (
        (blocks[0].astype(F32) + from_across.astype(F32))
        + (from_before.astype(F32) + from_after.astype(F32))
    )


def rotate(stack, start):
    return lax.dynamic_slice_in_dim(jnp.concatenate([stack, stack], 0), start, 4, 0)


def params():
    return pltpu.CompilerParams(vmem_limit_bytes=VMEM_LIMIT)


def project(order, own, other, pieces):
    rows = own.shape[0]

    def kernel(order_ref, own_ref, other_ref, r0, r1, r2, r3, out_own, out_other, squares, acc):
        step = pl.program_id(0)

        @pl.when(step == 0)
        def _():
            acc[...] = jnp.zeros_like(acc)

        for k, ref in enumerate((r0, r1, r2, r3)):

            @pl.when(step // 4 == k)
            def _(ref=ref):
                acc[0] += jnp.dot(own_ref[...], ref[0], preferred_element_type=F32)
                acc[1] += jnp.dot(other_ref[...], ref[0], preferred_element_type=F32)

        @pl.when(step == 15)
        def _():
            out_own[...] = acc[0]
            out_other[...] = acc[1].astype(BF)
            squares[...] = jnp.sum(acc[0] * acc[0] + acc[1] * acc[1], axis=0, keepdims=True)

    def piece_spec(k):
        return pl.BlockSpec(
            (1, UNIT, HALF), lambda i, order: (jnp.clip(i - 4 * k, 0, 3), 0, 0)
        )

    column = pl.BlockSpec((rows, UNIT), lambda i, order: (0, order[i]))
    whole = lambda shape: pl.BlockSpec(shape, lambda i, order: (0, 0))
    return pl.pallas_call(
        kernel,
        grid_spec=pltpu.PrefetchScalarGridSpec(
            num_scalar_prefetch=1,
            grid=(16,),
            in_specs=[column, column] + [piece_spec(k) for k in range(4)],
            out_specs=[whole((rows, HALF)), whole((rows, HALF)), whole((1, HALF))],
            scratch_shapes=[pltpu.VMEM((2, rows, HALF), F32)],
        ),
        out_shape=[
            jax.ShapeDtypeStruct((rows, HALF), F32),
            jax.ShapeDtypeStruct((rows, HALF), BF),
            jax.ShapeDtypeStruct((1, HALF), F32),
        ],
        compiler_params=params(),
    )(order, own, other, *pieces)


def project_back(order, own, other, p_own, p_other):
    rows = own.shape[0]
    contract = (((0,), (0,)), ((), ()))

    def kernel(order_ref, own_ref, other_ref, p_own_ref, p_other_ref, q0, q1, q2, q3):
        step = pl.program_id(0)
        value = lax.dot_general(p_own_ref[...], own_ref[...], contract, preferred_element_type=F32)
        value += lax.dot_general(
            p_other_ref[...], other_ref[...], contract, preferred_element_type=F32
        )
        value = value.astype(BF)
        for k, ref in enumerate((q0, q1, q2, q3)):

            @pl.when(step // 4 == k)
            def _(ref=ref):
                ref[0] = value

    column = pl.BlockSpec((rows, UNIT), lambda i, order: (0, order[i]))
    whole = pl.BlockSpec((rows, HALF), lambda i, order: (0, 0))

    def slab_spec(k):
        return pl.BlockSpec(
            (1, HALF, UNIT), lambda i, order: (jnp.clip(i - 4 * k, 0, 3), 0, 0)
        )

    return pl.pallas_call(
        kernel,
        grid_spec=pltpu.PrefetchScalarGridSpec(
            num_scalar_prefetch=1,
            grid=(16,),
            in_specs=[column, column, whole, whole],
            out_specs=[slab_spec(k) for k in range(4)],
        ),
        out_shape=[jax.ShapeDtypeStruct((4, HALF, UNIT), BF)] * 4,
        compiler_params=params(),
    )(order, own, other, p_own, p_other)


def update_momentum(where_own, where_other, momentum, gradient, left_own, left_other, q_own, q_other):
    rows, width = momentum.shape

    def kernel(a_ref, b_ref, m_ref, g_ref, lo_ref, lp_ref, qo_ref, qp_ref, out_ref):
        change = jnp.dot(lo_ref[...], qo_ref[0], preferred_element_type=F32)
        change += jnp.dot(lp_ref[...], qp_ref[0], preferred_element_type=F32)
        out_ref[...] = (m_ref[...] + g_ref[...].astype(F32)) - change

    column = pl.BlockSpec((rows, UNIT), lambda i, a, b: (0, i))
    whole = pl.BlockSpec((rows, HALF), lambda i, a, b: (0, 0))
    return pl.pallas_call(
        kernel,
        grid_spec=pltpu.PrefetchScalarGridSpec(
            num_scalar_prefetch=2,
            grid=(16,),
            in_specs=[
                column,
                column,
                whole,
                whole,
                pl.BlockSpec((1, HALF, UNIT), lambda i, a, b: (a[i], 0, 0)),
                pl.BlockSpec((1, HALF, UNIT), lambda i, a, b: (b[i], 0, 0)),
            ],
            out_specs=column,
        ),
        out_shape=jax.ShapeDtypeStruct((rows, width), F32),
        compiler_params=params(),
    )(where_own, where_other, momentum, gradient, left_own, left_other, q_own, q_other)


def shards(momentum, gradient, right_basis, weight, tokens):
    row, col = lax.axis_index("row"), lax.axis_index("col")
    x, y, z, core = row // 2, (col // 8) * 2 + row % 2, (col // 2) % 4, col % 2
    first = core == 0
    total_rows = momentum.shape[0] * 128
    rank = right_basis.shape[1]
    width = momentum.shape[1]
    big, middle = ("x", "y"), ("y", "x")
    deep = ("z", "z")

    i = jnp.arange(16, dtype=jnp.int32)

    def unit_at(core_is_first):
        far, near = i // 4, i % 4
        ux = jnp.where(core_is_first, x + far, x + near) % 4
        uy = jnp.where(core_is_first, y + near, y + far) % 4
        return (ux * 4 + (uy % 2) * 2 + uy // 2).astype(jnp.int32)

    def place_of(core_is_first):
        ux, uy = i // 4, (i % 2) * 2 + (i // 2) % 2
        dx, dy = (ux - x) % 4, (uy - y) % 4
        return jnp.where(core_is_first, dx * 4 + dy, dy * 4 + dx).astype(jnp.int32)

    order = unit_at(first)
    where_own, where_other = place_of(first), place_of(jnp.logical_not(first))

    def halves(a):
        low, high = a[:, :HALF], a[:, HALF:]
        return jnp.where(first, low, high), jnp.where(first, high, low)

    def by_core(mine, theirs):
        return jnp.where(first, mine, theirs), jnp.where(first, theirs, mine)

    basis_own, basis_sent = halves(right_basis)
    basis_chip = jnp.concatenate(by_core(basis_own, swap_cores(basis_sent)), 0)
    stack = jnp.stack(gather_ring(basis_chip, deep))
    unit = rotate(stack, (4 - z) % 4).reshape(UNIT, HALF)
    slab = jnp.stack(gather_ring(unit, middle))
    pieces = gather_ring(slab, big)

    buffer_low = (momentum + gradient.astype(F32)).astype(BF)
    buffer_other = swap_cores(buffer_low)
    tokens_all = lax.all_gather(tokens, "col", axis=0, tiled=True)

    p_own, p_other, squares = project(order, buffer_low, buffer_other, pieces)
    p_own_low = p_own.astype(BF)
    p_from_other = swap_cores(p_other)

    p_tile = lax.all_gather(jnp.stack(by_core(p_own_low, p_other)), "col", axis=0,
                            axis_index_groups=[[c + 2 * k for k in range(8)] for c in range(2)], tiled=True)
    p_tile = p_tile.reshape(-1, HALF)
    p_tile_other = swap_cores(p_tile)

    slabs = project_back(order, buffer_low, buffer_other, p_own_low, p_other)
    chips = [[2 * k + c for k in range(64)] for c in range(2)]

    def total(part):
        parts = lax.all_to_all(jnp.broadcast_to(part[None], (64, 1, HALF)), ALL, 0, 0,
                               axis_index_groups=chips, tiled=True)
        return jnp.sum(parts, axis=(0, 1))

    p_squares = total(squares)
    scale = lax.rsqrt(p_squares + EPSILON)
    summed = scatter_ring(slabs, big).astype(BF)
    summed = scatter_ring([summed[k] for k in range(4)], middle).astype(BF)
    summed = summed.reshape(HALF, 4, 128).transpose(1, 0, 2)
    summed = rotate(summed, z)
    q_block = scatter_ring([summed[k] for k in range(4)], deep).astype(BF)

    q_wide = q_block.astype(F32)
    q_squares = total(jnp.sum(q_wide * q_wide, axis=1)[None])
    stack = rotate(jnp.stack(gather_ring(q_block, deep)), (4 - z) % 4)
    unit = stack.transpose(1, 0, 2).reshape(HALF, UNIT)
    slab = jnp.stack(gather_ring(unit, middle))
    q_own = jnp.concatenate(gather_ring(slab, big), 0)
    q_other = swap_cores(q_own)

    basis_scale = lax.rsqrt(scale * scale * q_squares + EPSILON)
    scales = jnp.stack([scale, basis_scale])
    scales_other = swap_cores(scales)

    factor = 1.0 - MOMENTUM_DECAY
    left_own = (p_own * (factor * scale * scale)).astype(BF)
    left_other = (p_from_other.astype(F32) * (factor * scales_other[0] * scales_other[0])).astype(BF)
    new_momentum = update_momentum(
        where_own, where_other, momentum, gradient, left_own, left_other, q_own, q_other
    )

    basis_block = q_wide * (scale * basis_scale)[:, None]
    low, high = basis_block[:, :64], basis_block[:, 64:]
    mine = jnp.where(first, low, high).T.astype(BF)
    theirs = jnp.where(first, high, low).T.astype(BF)
    new_basis = jnp.concatenate(by_core(mine, swap_cores(theirs)), 1)

    step_scale = STEP_SIZE * math.sqrt(total_rows * width / rank)
    tile_own = lax.dynamic_index_in_dim(q_own, where_own[col], 0, keepdims=False).astype(F32)
    tile_other = lax.dynamic_index_in_dim(q_other, where_other[col], 0, keepdims=False).astype(F32)
    tile_own = (tile_own * (step_scale * scale * scale * basis_scale)[:, None]).astype(BF)
    tile_other = (
        tile_other * (step_scale * scales_other[0] * scales_other[0] * scales_other[1])[:, None]
    ).astype(BF)
    change = jnp.dot(p_tile, tile_own, preferred_element_type=F32) + jnp.dot(
        p_tile_other, tile_other, preferred_element_type=F32
    )
    new_weight = (weight.astype(F32) - change).astype(BF)

    early = jnp.concatenate(
        [
            jnp.dot(tokens_all, weight, preferred_element_type=F32),
            jnp.dot(tokens_all, p_tile, preferred_element_type=F32),
            jnp.dot(tokens_all, p_tile_other, preferred_element_type=F32),
        ],
        1,
    )
    early = lax.psum_scatter(early, "row", scatter_dimension=0, tiled=True)
    tokens_left = early[:, UNIT:].astype(BF)
    late = jnp.dot(tokens_left[:, :HALF], tile_own, preferred_element_type=F32) + jnp.dot(
        tokens_left[:, HALF:], tile_other, preferred_element_type=F32
    )
    logits = ((early[:, :UNIT] - late) * total_rows ** (-0.5)).astype(BF)
    return (new_momentum, new_basis, new_weight, logits)


def solution(mesh):
    in_specs = (
        P(("row", "col"), None),
        P(("row", "col"), None),
        P(("row", "col"), None),
        P("row", "col"),
        P("col", "row"),
    )
    out_specs = (P(("row", "col"), None), P(("row", "col"), None), P("row", "col"), P("row", "col"))
    return jax.shard_map(shards, mesh=mesh, in_specs=in_specs, out_specs=out_specs, check_vma=False)
```

time: 1320 us -> 301 us (0.23)
  waiting for transfers between devices: 1110 us -> 121 us
  blocking collectives: 128 us -> 0 us
  starting transfers between devices: 0.24 us -> 66 us
  Pallas kernels: 0 us -> 41 us
  matrix products: 46.9 us -> 21.1 us
    reduce_scatter x1, waiting for transfers between devices: 654 us -> 0.01 us  [shards(): early = lax.psum_scatter(early, 'row', scatter_dimension=0, tiled=True)]
    all_gather x4 -> x2, waiting for transfers between devices: 435 us -> 0.01 us  [the longest x1 0.01 us: shards(): lax.all_gather(jnp.stack(by_core(p_own_low, p_other)), 'col', axis=0, axi...]
    psum x2 -> x0, blocking collectives: 128 us -> none  [the longest x1 64.2 us: shards(): lax.psum(jnp.sum(own_wide * own_wide, axis=0), ('row', 'col'))]
    ppermute x0 -> x34, waiting for transfers between devices: none -> 108 us  [the longest x27 101 us: shift_by(): return lax.ppermute(value, ALL, pairs)]
    ppermute x0 -> x34, starting transfers between devices: none -> 51.6 us  [the longest x27 41.3 us: shift_by(): return lax.ppermute(value, ALL, pairs)]
    pallas_call x0 -> x3, Pallas kernels: none -> 41 us  [the longest x1 15.6 us: update_momentum(): pl.pallas_call(kernel, grid_spec=pltpu.PrefetchScalarGridSpec(num_scalar_...]
    dot_general x5 -> x7, matrix products: 46.9 us -> 21.1 us  [the longest x1 6.09 us: shards(): jnp.dot(p_tile_other, tile_other, preferred_element_type=F32)]
    unnamed x7 -> x3, waiting for transfers between devices: 19.3 us -> 0.73 us
  transfers between devices with their start and end apart: 6 -> 39, of which waited for: 6 -> 25; matrix products, arithmetic and copies ran while one was open for 3% -> 14% of each run, Pallas kernels for 0% -> 9%
where the time goes in v1:
time: 301 us; the launch traced here: 300 us
  waiting for transfers between devices  121 us (40%)
  starting transfers between devices  66 us (22%)
  Pallas kernels  41 us (14%)
  matrix products  21.1 us (7%)
  local copies, waits for them, and re-layouts  20.6 us (7%)
  between operations  18.1 us (6%)
  other arithmetic  11.6 us (4%)
    ppermute x27, waiting for transfers between devices, shift_by(): return lax.ppermute(value, ALL, pairs)  101 us
    ppermute x27, starting transfers between devices, shift_by(): return lax.ppermute(value, ALL, pairs)  41.3 us
    pallas_call x1, Pallas kernels, update_momentum(): pl.pallas_call(kernel, grid_spec=pltpu.PrefetchScalarGridSpec(num_scalar_...  15.6 us
    all_to_all x2, starting transfers between devices, total(): lax.all_to_all(jnp.broadcast_to(part[None], (64, 1, HALF)), ALL, 0, 0, ax...  14.3 us
    unnamed x29, local copies, waits for them, and re-layouts  13.5 us
    pallas_call x1, Pallas kernels, project_back(): pl.pallas_call(kernel, grid_spec=pltpu.PrefetchScalarGridSpec(num_scalar_...  12.8 us
    pallas_call x1, Pallas kernels, project(): pl.pallas_call(kernel, grid_spec=pltpu.PrefetchScalarGridSpec(num_scalar_...  12.7 us
    all_to_all x2, waiting for transfers between devices, total(): lax.all_to_all(jnp.broadcast_to(part[None], (64, 1, HALF)), ALL, 0, 0, ax...  12.2 us
  transfers between devices with their start and end apart: 39, of which 25 were waited for; matrix products, arithmetic and copies ran while one was open for 14% of the time, Pallas kernels for 9%

profile of v1, /device:TPU:1, one launch (start us, length us, event | category | flops | bytes accessed | tf_op | source)
XLA Modules:
  0.0 299.9 jit_solution(174140132911501711)
XLA Ops:
  7.2 7.1 %add_convert_fusion.own_ref = bf16[231,8192]{1,0:T(8,128)(2,1)} fusion(f32[231,8192]{1,0:T(8,128)} %m_ref.1, bf16[231,8192]{1,0:T(8,128)(2,1)} %g_ref.1), kind=kLoop, calls=%fused_computation | loop fusion | flops 5677056 | bytes 15138816 | tf_op jit(solution)/shard_map/convert_element_type | solution.py:226
  15.9 6.0 %collective-permute-done.1 = bf16[64,256]{1,0:T(8,128)(2,1)S(1)} collective-permute-done((bf16[64,256]{1,0:T(8,128)(2,1)S(1)}, bf16[64,256]{1,0:T(8,128)(2,1)S(1)}, u32[]{:S(2)}, u32[]{:S(2)}) %collective-permute-start.1) | collective-permute-done | bytes 32800 | tf_op jit(solution)/shard_map/ppermute | solution.py:42
  21.9 3.8 %collective-permute-start.3 = (bf16[128,256]{1,0:T(8,128)(2,1)S(1)}, bf16[128,256]{1,0:T(8,128)(2,1)S(1)}, u32[]{:S(2)}, u32[]{:S(2)}) collective-permute-start(bf16[128,256]{1,0:T(8,128)(2,1)S(1)} %pad_maximum_fusion.4), channel_id=1, source_target_pairs={{0,4},{1,5},{2,6},{3,7},{4,0},{5,1},{6,2},{7,3},{16,20},{17,21},{1... | collective-permute-start | bytes 196616 | tf_op jit(solution)/shard_map/ppermute | solution.py:38
  37.3 3.8 %collective-permute-done.6 = bf16[512,256]{1,0:T(8,128)(2,1)S(1)} collective-permute-done((bf16[512,256]{1,0:T(8,128)(2,1)S(1)}, bf16[512,256]{1,0:T(8,128)(2,1)S(1)}, u32[]{:S(2)}, u32[]{:S(2)}) %collective-permute-start.6) | collective-permute-done | bytes 262176 | tf_op jit(solution)/shard_map/ppermute | solution.py:38
  46.0 10.4 %collective-permute-done.10.r3 = bf16[4,512,256]{2,1,0:T(8,128)(2,1)S(1)} collective-permute-done((bf16[4,512,256]{2,1,0:T(8,128)(2,1)S(1)}, bf16[4,512,256]{2,1,0:T(8,128)(2,1)S(1)}, u32[]{:S(2)}, u32[]{:S(2)}) %collective-permute-start.10) | collective-permute-done | bytes 1048608 | tf_op jit(solution)/shard_map/ppermute | solution.py:38
  56.4 12.2 %collective-permute-done.9.r2 = bf16[4,512,256]{2,1,0:T(8,128)(2,1)S(1)} collective-permute-done((bf16[4,512,256]{2,1,0:T(8,128)(2,1)S(1)}, bf16[4,512,256]{2,1,0:T(8,128)(2,1)S(1)}, u32[]{:S(2)}, u32[]{:S(2)}) %collective-permute-start.9) | collective-permute-done | bytes 1048608 | tf_op jit(solution)/shard_map/ppermute | solution.py:38
  68.6 12.7 %shard_map.84 = (f32[231,256]{1,0:T(8,128)S(1)}, bf16[231,256]{1,0:T(8,128)(2,1)S(1)}, f32[1,256]{1,0:T(1,128)S(1)}) custom-call(s32[16]{0:T(128)S(1)} %fusion.41.order_ref, bf16[231,8192]{1,0:T(8,128)(2,1)} %add_convert_fusion.own_ref, bf16[231,8192]{1,0:T(8,128)(2,1)} %collective-permute-done.other_ref, bf16[4,512,256]{2,1,0:T(8,128)(2,1)S(1)} %pad_maximum_fusion.1.r0, ...), custom_call_target="tpu_custom_call" | custom-call | tf_op jit(solution)/shard_map/pallas_call | solution.py:100
  82.9 12.8 %shard_map.85 = (bf16[4,256,512]{2,1,0:T(8,128)(2,1)S(1)}, bf16[4,256,512]{2,1,0:T(8,128)(2,1)S(1)}, bf16[4,256,512]{2,1,0:T(8,128)(2,1)S(1)}, bf16[4,256,512]{2,1,0:T(8,128)(2,1)S(1)}) custom-call(s32[16]{0:T(128)S(1)} %fusion.41.order_ref, bf16[231,8192]{1,0:T(8,128)(2,1)} %add_convert_fusion.own_ref, bf16[231,8192]{1,0:T(8,128)(2,1)} %collective-permute-done.other_ref, ...), custom_call_target="tpu_custom_call" | custom-call | tf_op jit(solution)/shard_map/pallas_call | solution.py:143
  100.9 12.1 %collective-permute-done.12 = bf16[4,256,512]{2,1,0:T(8,128)(2,1)S(1)} collective-permute-done((bf16[4,256,512]{2,1,0:T(8,128)(2,1)S(1)}, bf16[4,256,512]{2,1,0:T(8,128)(2,1)S(1)}, u32[]{:S(2)}, u32[]{:S(2)}) %collective-permute-start.12) | collective-permute-done | bytes 1048608 | tf_op jit(solution)/shard_map/ppermute | solution.py:38
  113.0 17.7 %collective-permute-done.13 = bf16[4,256,512]{2,1,0:T(8,128)(2,1)S(1)} collective-permute-done((bf16[4,256,512]{2,1,0:T(8,128)(2,1)S(1)}, bf16[4,256,512]{2,1,0:T(8,128)(2,1)S(1)}, u32[]{:S(2)}, u32[]{:S(2)}) %collective-permute-start.13) | collective-permute-done | bytes 1048608 | tf_op jit(solution)/shard_map/ppermute | solution.py:38
  131.3 2.9 collective-permute-start.15
  138.1 3.4 %collective-permute-done.17 = bf16[256,512]{1,0:T(8,128)(2,1)S(1)} collective-permute-done((bf16[256,512]{1,0:T(8,128)(2,1)S(1)}, bf16[256,512]{1,0:T(8,128)(2,1)S(1)}, u32[]{:S(2)}, u32[]{:S(2)}) %collective-permute-start.17) | collective-permute-done | bytes 262176 | tf_op jit(solution)/shard_map/ppermute | solution.py:38
  152.5 3.5 %collective-permute-done.23 = bf16[256,128]{0,1:T(8,128)(2,1)S(1)} collective-permute-done((bf16[256,128]{0,1:T(8,128)(2,1)S(1)}, bf16[256,128]{0,1:T(8,128)(2,1)S(1)}, u32[]{:S(2)}, u32[]{:S(2)}) %collective-permute-start.23) | collective-permute-done | bytes 65568 | tf_op jit(solution)/shard_map/ppermute | solution.py:38
  163.4 3.0 %collective-permute-done.26 = bf16[256,512]{1,0:T(8,128)(2,1)S(1)} collective-permute-done((bf16[256,512]{1,0:T(8,128)(2,1)S(1)}, bf16[256,512]{1,0:T(8,128)(2,1)S(1)}, u32[]{:S(2)}, u32[]{:S(2)}) %collective-permute-start.26) | collective-permute-done | bytes 262176 | tf_op jit(solution)/shard_map/ppermute | solution.py:38
  166.9 4.1 %collective-permute-start.28 = (bf16[4,256,512]{2,1,0:T(8,128)(2,1)S(1)}, bf16[4,256,512]{2,1,0:T(8,128)(2,1)}, u32[]{:S(2)}, u32[]{:S(2)}) collective-permute-start(bf16[4,256,512]{2,1,0:T(8,128)(2,1)S(1)} %pad_maximum_fusion.2), channel_id=1, source_target_pairs={{0,96},{1,25},{2,98},{3,27},{4,100},{5,29},{6,102},{7,31},{16,112}... | collective-permute-start | bytes 3145736 | tf_op jit(solution)/shard_map/ppermute | solution.py:38
  175.2 3.9 %collective-permute-start.33 = (bf16[3696,256]{1,0:T(8,128)(2,1)S(1)}, bf16[3696,256]{1,0:T(8,128)(2,1)}, u32[]{:S(2)}, u32[]{:S(2)}) collective-permute-start(bf16[3696,256]{1,0:T(8,128)(2,1)S(1)} %reshape.114), channel_id=1, source_target_pairs={{0,1},{1,0},{2,3},{3,2},{4,5},{5,4},{6,7},{7,6},{8,9},{9,8},{10,11... | collective-permute-start | bytes 5677064 | tf_op jit(solution)/shard_map/ppermute | solution.py:42
  182.5 21.7 %collective-permute-done.28 = bf16[4,256,512]{2,1,0:T(8,128)(2,1)} collective-permute-done((bf16[4,256,512]{2,1,0:T(8,128)(2,1)S(1)}, bf16[4,256,512]{2,1,0:T(8,128)(2,1)}, u32[]{:S(2)}, u32[]{:S(2)}) %collective-permute-start.28) | collective-permute-done | bytes 1048608 | tf_op jit(solution)/shard_map/ppermute | solution.py:38
  211.1 5.6 %fusion.51 = f32[512,512]{0,1:T(8,128)S(1)} fusion(bf16[512,3696]{1,0:T(8,128)(2,1)} %all-gather.5.cloned.1.call-done, bf16[3696,512]{1,0:T(8,128)(2,1)} %param.8), kind=kOutput, calls=%fused_computation.153 | convolution fusion | flops 1937768448 | bytes 8617984 | tf_op jit(solution)/shard_map/dot_general | solution.py:294
  227.7 9.3 %all-to-all-start = ((f32[64,1,256]{2,1,0:T(1,128)}), f32[64,1,256]{2,1,0:T(1,128)S(1)}, u32[]{:S(2)}, u32[]{:S(2)}) async-start(f32[64,1,256]{2,1,0:T(1,128)} %broadcast_in_dim.7), calls=%async_computation | async-start | bytes 131072 | tf_op jit(solution)/shard_map/all_to_all | solution.py:243
  237.1 8.7 %all-to-all-done = f32[64,1,256]{2,1,0:T(1,128)S(1)} async-done(((f32[64,1,256]{2,1,0:T(1,128)}), f32[64,1,256]{2,1,0:T(1,128)S(1)}, u32[]{:S(2)}, u32[]{:S(2)}) %all-to-all-start) | async-done | bytes 65568 | tf_op jit(solution)/shard_map/all_to_all | solution.py:243
  246.5 5.0 %all-to-all-start.1 = ((f32[64,1,256]{2,1,0:T(1,128)}), f32[64,1,256]{2,1,0:T(1,128)S(1)}, u32[]{:S(2)}, u32[]{:S(2)}) async-start(f32[64,1,256]{2,1,0:T(1,128)} %broadcast_in_dim.8), calls=%async_computation.1 | async-start | bytes 131072 | tf_op jit(solution)/shard_map/all_to_all | solution.py:243
  256.5 3.5 %all-to-all-done.1 = f32[64,1,256]{2,1,0:T(1,128)S(1)} async-done(((f32[64,1,256]{2,1,0:T(1,128)}), f32[64,1,256]{2,1,0:T(1,128)S(1)}, u32[]{:S(2)}, u32[]{:S(2)}) %all-to-all-start.1) | async-done | bytes 65568 | tf_op jit(solution)/shard_map/all_to_all | solution.py:243
  267.5 15.6 %shard_map.86 = f32[231,8192]{1,0:T(8,128)} custom-call(s32[16]{0:T(128)S(1)} %broadcast_select_fusion.9.a_ref, s32[16]{0:T(128)S(1)} %broadcast_select_fusion.6.b_ref, f32[231,8192]{1,0:T(8,128)} %m_ref.1, bf16[231,8192]{1,0:T(8,128)(2,1)S(1)} %copy-done, bf16[231,256]{1,0:T(8,128)(2,1)S(1)} %multiply_convert_fusion.1.lo_ref, ...), custom_call_target="tpu_custom_call" | custom-call | tf_op jit(solution)/shard_map/pallas_call | solution.py:166
  283.1 6.1 %subtract_convert_fusion = bf16[3696,512]{1,0:T(8,128)(2,1)} fusion(f32[3696,512]{1,0:T(8,128)S(1)} %fusion.10, bf16[3696,512]{1,0:T(8,128)(2,1)} %param.8, bf16[3696,256]{1,0:T(8,128)(2,1)} %collective-permute-done.33, f32[256]{0:T(256)S(1)} %fusion.34, bf16[16,256,512]{2,1,0:T(8,128)(2,1)} %collective-permute-done.31.qp_ref, s32[]{:T(128)S(6)} %select_n.226), kind=kOutput, calls=%fused_computation.1 | convolution fusion | flops 976846848 | bytes 17294340 | tf_op jit(solution)/shard_map/dot_general | solution.py:287
  (145 shorter events, 87.0 us)
Async XLA Ops:
  7.2 166.2 %all-gather.3.cloned.1.call-start = ((), (), s32[]{:S(2)}) async-start(), calls=%async_computation.3 | async-start | bytes 2138112 | tf_op jit(solution)/shard_map/all_gather | solution.py:234
  14.3 54.3 %collective-permute-start = (bf16[231,8192]{1,0:T(8,128)(2,1)}, bf16[231,8192]{1,0:T(8,128)(2,1)}, u32[]{:S(2)}, u32[]{:S(2)}) collective-permute-start(bf16[231,8192]{1,0:T(8,128)(2,1)} %add_convert_fusion.own_ref), channel_id=1, source_target_pairs={{0,1},{1,0},{2,3},{3,2},{4,5},{5,4},{6,7},{7,6},{8,9},{9,8},{10,11... | collective-permute-start | bytes 11354120 | tf_op jit(solution)/shard_map/ppermute | solution.py:42
  21.9 8.0 %collective-permute-start.3 = (bf16[128,256]{1,0:T(8,128)(2,1)S(1)}, bf16[128,256]{1,0:T(8,128)(2,1)S(1)}, u32[]{:S(2)}, u32[]{:S(2)}) collective-permute-start(bf16[128,256]{1,0:T(8,128)(2,1)S(1)} %pad_maximum_fusion.4), channel_id=1, source_target_pairs={{0,4},{1,5},{2,6},{3,7},{4,0},{5,1},{6,2},{7,3},{16,20},{17,21},{1... | collective-permute-start | bytes 196616 | tf_op jit(solution)/shard_map/ppermute | solution.py:38
  31.8 9.3 %collective-permute-start.6 = (bf16[512,256]{1,0:T(8,128)(2,1)S(1)}, bf16[512,256]{1,0:T(8,128)(2,1)S(1)}, u32[]{:S(2)}, u32[]{:S(2)}) collective-permute-start(bf16[512,256]{1,0:T(8,128)(2,1)S(1)} %bitcast.118), channel_id=1, source_target_pairs={{0,8},{1,65},{2,10},{3,67},{4,12},{5,69},{6,14},{7,71},{16,24},{17... | collective-permute-start | bytes 786440 | tf_op jit(solution)/shard_map/ppermute | solution.py:38
  41.2 15.2 %collective-permute-start.10 = (bf16[4,512,256]{2,1,0:T(8,128)(2,1)S(1)}, bf16[4,512,256]{2,1,0:T(8,128)(2,1)S(1)}, u32[]{:S(2)}, u32[]{:S(2)}) collective-permute-start(bf16[4,512,256]{2,1,0:T(8,128)(2,1)S(1)} %pad_maximum_fusion.1.r0), channel_id=1, source_target_pairs={{0,32},{1,17},{2,34},{3,19},{4,36},{5,21},{6,38},{7,23},{16,48},{1... | collective-permute-start | bytes 3145736 | tf_op jit(solution)/shard_map/ppermute | solution.py:38
  42.3 26.3 %collective-permute-start.9 = (bf16[4,512,256]{2,1,0:T(8,128)(2,1)S(1)}, bf16[4,512,256]{2,1,0:T(8,128)(2,1)S(1)}, u32[]{:S(2)}, u32[]{:S(2)}) collective-permute-start(bf16[4,512,256]{2,1,0:T(8,128)(2,1)S(1)} %pad_maximum_fusion.1.r0), channel_id=1, source_target_pairs={{0,64},{1,9},{2,66},{3,11},{4,68},{5,13},{6,70},{7,15},{16,80},{17... | collective-permute-start | bytes 3145736 | tf_op jit(solution)/shard_map/ppermute | solution.py:38
  44.9 23.7 %collective-permute-start.8 = (bf16[4,512,256]{2,1,0:T(8,128)(2,1)S(1)}, bf16[4,512,256]{2,1,0:T(8,128)(2,1)}, u32[]{:S(2)}, u32[]{:S(2)}) collective-permute-start(bf16[4,512,256]{2,1,0:T(8,128)(2,1)S(1)} %pad_maximum_fusion.1.r0), channel_id=1, source_target_pairs={{0,96},{1,25},{2,98},{3,27},{4,100},{5,29},{6,102},{7,31},{16,112}... | collective-permute-start | bytes 3145736 | tf_op jit(solution)/shard_map/ppermute | solution.py:38
  82.1 128.9 %all-gather.5.cloned.1.call-start = ((), (), s32[]{:S(2)}) async-start(), calls=%async_computation.4 | async-start | bytes 4038656 | tf_op jit(solution)/shard_map/all_gather | solution.py:228
  82.9 206.3 %reduce-scatter.4.cloned.1.call-start = ((), (), s32[]{:S(2)}) async-start(), calls=%async_computation.5 | async-start | bytes 2359296 | tf_op jit(solution)/shard_map/reduce_scatter | solution.py:300
  95.7 17.3 %collective-permute-start.12 = (bf16[4,256,512]{2,1,0:T(8,128)(2,1)S(1)}, bf16[4,256,512]{2,1,0:T(8,128)(2,1)S(1)}, u32[]{:S(2)}, u32[]{:S(2)}) collective-permute-start(bf16[4,256,512]{2,1,0:T(8,128)(2,1)S(1)} %get-tuple-element.15), channel_id=1, source_target_pairs={{0,64},{1,9},{2,66},{3,11},{4,68},{5,13},{6,70},{7,15},{16,80},{17... | collective-permute-start | bytes 3145736 | tf_op jit(solution)/shard_map/ppermute | solution.py:38
  98.2 32.5 %collective-permute-start.13 = (bf16[4,256,512]{2,1,0:T(8,128)(2,1)S(1)}, bf16[4,256,512]{2,1,0:T(8,128)(2,1)S(1)}, u32[]{:S(2)}, u32[]{:S(2)}) collective-permute-start(bf16[4,256,512]{2,1,0:T(8,128)(2,1)S(1)} %get-tuple-element.16), channel_id=1, source_target_pairs={{0,32},{1,17},{2,34},{3,19},{4,36},{5,21},{6,38},{7,23},{16,48},{1... | collective-permute-start | bytes 3145736 | tf_op jit(solution)/shard_map/ppermute | solution.py:38
  98.4 32.3 %collective-permute-start.14 = (bf16[4,256,512]{2,1,0:T(8,128)(2,1)S(1)}, bf16[4,256,512]{2,1,0:T(8,128)(2,1)S(1)}, u32[]{:S(2)}, u32[]{:S(2)}) collective-permute-start(bf16[4,256,512]{2,1,0:T(8,128)(2,1)S(1)} %get-tuple-element.17), channel_id=1, source_target_pairs={{0,96},{1,25},{2,98},{3,27},{4,100},{5,29},{6,102},{7,31},{16,112}... | collective-permute-start | bytes 3145736 | tf_op jit(solution)/shard_map/ppermute | solution.py:38
  134.3 7.3 %collective-permute-start.17 = (bf16[256,512]{1,0:T(8,128)(2,1)S(1)}, bf16[256,512]{1,0:T(8,128)(2,1)S(1)}, u32[]{:S(2)}, u32[]{:S(2)}) collective-permute-start(bf16[256,512]{1,0:T(8,128)(2,1)S(1)} %get-tuple-element.33), channel_id=1, source_target_pairs={{0,24},{1,97},{2,26},{3,99},{4,28},{5,101},{6,30},{7,103},{16,0},{... | collective-permute-start | bytes 786440 | tf_op jit(solution)/shard_map/ppermute | solution.py:38
  156.3 7.1 %collective-permute-start.27 = (bf16[256,512]{1,0:T(8,128)(2,1)S(1)}, bf16[256,512]{1,0:T(8,128)(2,1)S(1)}, u32[]{:S(2)}, u32[]{:S(2)}) collective-permute-start(bf16[256,512]{1,0:T(8,128)(2,1)S(1)} %copy.37), channel_id=1, source_target_pairs={{0,16},{1,33},{2,18},{3,35},{4,20},{5,37},{6,22},{7,39},{16,8},{17... | collective-permute-start | bytes 786440 | tf_op jit(solution)/shard_map/ppermute | solution.py:38
  157.7 8.7 %collective-permute-start.26 = (bf16[256,512]{1,0:T(8,128)(2,1)S(1)}, bf16[256,512]{1,0:T(8,128)(2,1)S(1)}, u32[]{:S(2)}, u32[]{:S(2)}) collective-permute-start(bf16[256,512]{1,0:T(8,128)(2,1)S(1)} %copy.37), channel_id=1, source_target_pairs={{0,8},{1,65},{2,10},{3,67},{4,12},{5,69},{6,14},{7,71},{16,24},{17... | collective-permute-start | bytes 786440 | tf_op jit(solution)/shard_map/ppermute | solution.py:38
  159.8 6.9 %collective-permute-start.25 = (bf16[256,512]{1,0:T(8,128)(2,1)S(1)}, bf16[256,512]{1,0:T(8,128)(2,1)S(1)}, u32[]{:S(2)}, u32[]{:S(2)}) collective-permute-start(bf16[256,512]{1,0:T(8,128)(2,1)S(1)} %copy.37), channel_id=1, source_target_pairs={{0,24},{1,97},{2,26},{3,99},{4,28},{5,101},{6,30},{7,103},{16,0},{... | collective-permute-start | bytes 786440 | tf_op jit(solution)/shard_map/ppermute | solution.py:38
  166.9 37.3 %collective-permute-start.28 = (bf16[4,256,512]{2,1,0:T(8,128)(2,1)S(1)}, bf16[4,256,512]{2,1,0:T(8,128)(2,1)}, u32[]{:S(2)}, u32[]{:S(2)}) collective-permute-start(bf16[4,256,512]{2,1,0:T(8,128)(2,1)S(1)} %pad_maximum_fusion.2), channel_id=1, source_target_pairs={{0,96},{1,25},{2,98},{3,27},{4,100},{5,29},{6,102},{7,31},{16,112}... | collective-permute-start | bytes 3145736 | tf_op jit(solution)/shard_map/ppermute | solution.py:38
  171.0 35.4 %collective-permute-start.29 = (bf16[4,256,512]{2,1,0:T(8,128)(2,1)S(1)}, bf16[4,256,512]{2,1,0:T(8,128)(2,1)}, u32[]{:S(2)}, u32[]{:S(2)}) collective-permute-start(bf16[4,256,512]{2,1,0:T(8,128)(2,1)S(1)} %pad_maximum_fusion.2), channel_id=1, source_target_pairs={{0,64},{1,9},{2,66},{3,11},{4,68},{5,13},{6,70},{7,15},{16,80},{17... | collective-permute-start | bytes 3145736 | tf_op jit(solution)/shard_map/ppermute | solution.py:38
  171.3 37.4 %collective-permute-start.30 = (bf16[4,256,512]{2,1,0:T(8,128)(2,1)S(1)}, bf16[4,256,512]{2,1,0:T(8,128)(2,1)}, u32[]{:S(2)}, u32[]{:S(2)}) collective-permute-start(bf16[4,256,512]{2,1,0:T(8,128)(2,1)S(1)} %pad_maximum_fusion.2), channel_id=1, source_target_pairs={{0,32},{1,17},{2,34},{3,19},{4,36},{5,21},{6,38},{7,23},{16,48},{1... | collective-permute-start | bytes 3145736 | tf_op jit(solution)/shard_map/ppermute | solution.py:38
  175.2 42.8 %collective-permute-start.33 = (bf16[3696,256]{1,0:T(8,128)(2,1)S(1)}, bf16[3696,256]{1,0:T(8,128)(2,1)}, u32[]{:S(2)}, u32[]{:S(2)}) collective-permute-start(bf16[3696,256]{1,0:T(8,128)(2,1)S(1)} %reshape.114), channel_id=1, source_target_pairs={{0,1},{1,0},{2,3},{3,2},{4,5},{5,4},{6,7},{7,6},{8,9},{9,8},{10,11... | collective-permute-start | bytes 5677064 | tf_op jit(solution)/shard_map/ppermute | solution.py:42
  211.1 56.4 %collective-permute-start.31 = (bf16[16,256,512]{2,1,0:T(8,128)(2,1)}, bf16[16,256,512]{2,1,0:T(8,128)(2,1)}, u32[]{:S(2)}, u32[]{:S(2)}) collective-permute-start(bf16[16,256,512]{2,1,0:T(8,128)(2,1)} %constant_dynamic-update-slice_fusion.qo_ref), channel_id=1, source_target_pairs={{0,1},{1,0},{2,3},{3,2},{4,5},{5,4},{6,7},{7,6},{8,9},{9,8},{10,11... | collective-permute-start | bytes 12582920 | tf_op jit(solution)/shard_map/ppermute | solution.py:42
  227.7 18.1 %all-to-all-start = ((f32[64,1,256]{2,1,0:T(1,128)}), f32[64,1,256]{2,1,0:T(1,128)S(1)}, u32[]{:S(2)}, u32[]{:S(2)}) async-start(f32[64,1,256]{2,1,0:T(1,128)} %broadcast_in_dim.7), calls=%async_computation | async-start | bytes 131072 | tf_op jit(solution)/shard_map/all_to_all | solution.py:243
  246.5 13.5 %all-to-all-start.1 = ((f32[64,1,256]{2,1,0:T(1,128)}), f32[64,1,256]{2,1,0:T(1,128)S(1)}, u32[]{:S(2)}, u32[]{:S(2)}) async-start(f32[64,1,256]{2,1,0:T(1,128)} %broadcast_in_dim.8), calls=%async_computation.1 | async-start | bytes 131072 | tf_op jit(solution)/shard_map/all_to_all | solution.py:243
  254.7 9.0 %collective-permute-start.11 = (bf16[231,256]{1,0:T(8,128)(2,1)S(1)}, bf16[231,256]{1,0:T(8,128)(2,1)S(1)}, u32[]{:S(2)}, u32[]{:S(2)}) collective-permute-start(bf16[231,256]{1,0:T(8,128)(2,1)S(1)} %get-tuple-element.13.p_other_ref), channel_id=1, source_target_pairs={{0,1},{1,0},{2,3},{3,2},{4,5},{5,4},{6,7},{7,6},{8,9},{9,8},{10,11... | collective-permute-start | bytes 354824 | tf_op jit(solution)/shard_map/ppermute | solution.py:42
  (20 other events, 107.7 us)
Sparse Core Ops, SparseCore 0:
  82.3 60.7 all-gather.2
  145.5 56.9 all-gather.4
  225.2 51.5 reduce-scatter.3
